TPU v7x, 32 devices: a whole 2x2x4 slice. The times are simulated.
32 devices in a mesh: groups: 2 (over x), section: 2 (over core), tp: 8 (over z, y).
Axes of the slice: x: 2, y: 2, z: 4, core: 2. Of those that a mesh axis runs over, the one named last changes fastest.
Arguments:
- hidden: bfloat16 [2, 256, 8192], P('section', 'groups', 'tp'), parts along dimension 1, may hold values from -6 to 6
- norm_gain: float32 [2, 8192], P('section'), may hold values from 0.1 to 1.9
- w_query: bfloat16 [2, 8192, 8192], P('section', None, 'tp'), may hold values from -0.0625 to 0.0625
- key_value_weight: bfloat16 [2, 8192, 2048], P('section', None, 'tp'), may hold values from -0.0625 to 0.0625
- w_out: bfloat16 [2, 8192, 8192], P('section', 'tp'), may hold values from -0.875 to 0.875
- cache_pages: bfloat16 [2, 16384, 2048], P('section', ('groups', 'tp')), parts along dimension 1, may hold values from -260 to 260
- prefix_len: int32 [2, 2], P('section', 'groups'), parts along dimension 1, may hold values from 4096 to 8192, as said below
- page_owner: int32 [2, 32], P('section', 'groups'), parts along dimension 1, may hold values from 0 to 7, as said below
Outputs:
- handed: bfloat16 [2, 256, 8192], P('section', 'groups', 'tp'), parts along dimension 1
- pages_out: bfloat16 [2, 8, 8, 8, 2048], P('section', 'tp', 'groups'), parts along dimension 2
There are 2 independent parts, one for each index of `groups`. A program takes and returns all parts, laid end to end along the dimension named above; an argument that names none is the same for every part. Nothing has to cross between parts.
Inputs may be any that keep to these rules, and one draw needn't show every extreme that they name: `page_owner`: for each section at most 4 pages share an owner, and some owner has exactly 4. prefix_len of the first section is 8192.
All inputs are finite; a program needn't handle non-finite values.
Results may differ from a plain program's by a relative error of at most 0.028.
Values may be sent and summed in bfloat16 or wider, within the bound.
A program may use at most 128 MiB of HBM per device.

v0:
```python
import jax
import jax.numpy as jnp
import numpy as np
from jax import lax
from jax.sharding import PartitionSpec as P

QUERY_HEADS = 64
KEY_VALUE_HEADS = 8
HEAD_SIZE = 128
SPAN_TOKENS = 128
PAGE = 8
MOST = 4
NPAGE = 16


ROPE_BASE = 500000.0
NEG_FILL = -1e30


def passed_along(array, axis, by):
    length = lax.axis_size(axis)
    return lax.ppermute(array, axis, [(i, (i + by) % length) for i in range(length)])


def apply_rotary(values, token_places):
    head_width = values.shape[-1]
    half_width = head_width // 2
    inv_freq = ROPE_BASE ** (-jnp.arange(half_width, dtype=jnp.float32) * (2.0 / head_width))
    angles = token_places.astype(jnp.float32)[:, None] * inv_freq[None, :]
    cosine = jnp.cos(angles)[:, None, :]
    sine_part = jnp.sin(angles)[:, None, :]
    first_half = values[..., :half_width]
    second_half = values[..., half_width:]
    return jnp.concatenate(
        [
            first_half * cosine - second_half * sine_part,
            second_half * cosine + first_half * sine_part,
        ],
        axis=-1,
    )


def rotate_fresh(new_key_value, token_places):
    key_column_count = KEY_VALUE_HEADS * HEAD_SIZE
    rotary_output = apply_rotary(
        new_key_value[:, :key_column_count]
        .astype(jnp.float32)
        .reshape(-1, KEY_VALUE_HEADS, HEAD_SIZE),
        token_places,
    )
    return jnp.concatenate(
        [
            rotary_output.reshape(-1, key_column_count).astype(jnp.bfloat16),
            new_key_value[:, key_column_count:],
        ],
        axis=1,
    )


def fresh_pages(fresh_rot, owners, my_index):
    page_index = jnp.arange(NPAGE, dtype=jnp.int32)
    same_owner = owners[:, None] == owners[None, :]
    earlier = page_index[None, :] < page_index[:, None]
    page_rank = jnp.sum((same_owner & earlier).astype(jnp.int32), axis=1)
    slot_index = jnp.arange(MOST, dtype=jnp.int32)
    matched = (owners[None, :] == my_index) & (page_rank[None, :] == slot_index[:, None])
    flat_pages = fresh_rot.reshape(NPAGE, PAGE * fresh_rot.shape[1])
    picked = jnp.dot(
        matched.astype(jnp.bfloat16), flat_pages, preferred_element_type=jnp.float32
    ).astype(jnp.bfloat16)
    slot_page = jnp.sum(jnp.where(matched, page_index[None, :], 0), axis=1)
    slot_live = jnp.any(matched, axis=1)
    return (picked, slot_page, slot_live)


def on_device(
    hidden, norm_gain, w_query, key_value_weight, w_out, cache_pages, prefix_len, page_owner
):
    tp_size = lax.axis_size("tp")
    my_index = lax.axis_index("tp")
    heads_here = QUERY_HEADS // tp_size
    query_group_width = QUERY_HEADS // KEY_VALUE_HEADS
    key_column_count = KEY_VALUE_HEADS * HEAD_SIZE
    own_rows = hidden[0]
    full_rows = lax.all_gather(own_rows, "tp", axis=1, tiled=True)
    rows_f32 = full_rows.astype(jnp.float32)
    normed = (
        rows_f32
        * lax.rsqrt(jnp.mean(rows_f32 * rows_f32, axis=1, keepdims=True) + 1e-05)
        * norm_gain[0][None, :]
    ).astype(jnp.bfloat16)
    cached_len = prefix_len[0, 0]
    token_index = jnp.arange(SPAN_TOKENS, dtype=jnp.int32)
    token_places = cached_len + token_index
    query_f32 = jnp.dot(normed, w_query[0], preferred_element_type=jnp.float32).reshape(
        SPAN_TOKENS, heads_here, HEAD_SIZE
    )
    queries = (
        apply_rotary(query_f32, token_places)
        .astype(jnp.bfloat16)
        .reshape(SPAN_TOKENS, heads_here * HEAD_SIZE)
    )
    fresh_part = jnp.dot(normed, key_value_weight[0], preferred_element_type=jnp.float32).astype(
        jnp.bfloat16
    )
    cached = cache_pages[0]
    slots_here = cached.shape[0]
    head_table = np.arange(tp_size) * heads_here // query_group_width
    split_view = cached.reshape(slots_here, 2, KEY_VALUE_HEADS, HEAD_SIZE)[:, :, head_table, :]
    outgoing = jnp.transpose(split_view, (2, 0, 1, 3)).reshape(tp_size, slots_here, 2 * HEAD_SIZE)
    arrived = lax.all_to_all(outgoing, "tp", split_axis=0, concat_axis=0, tiled=True)
    fresh_all = lax.all_gather(fresh_part, "tp", axis=1, tiled=True)
    fresh_rot = rotate_fresh(fresh_all, token_places)
    picked, slot_page, slot_live = fresh_pages(fresh_rot, page_owner[0], my_index)
    kv_head = my_index * heads_here // query_group_width
    local_key_rows = lax.dynamic_slice_in_dim(fresh_rot, kv_head * HEAD_SIZE, HEAD_SIZE, 1)
    local_value_rows = lax.dynamic_slice_in_dim(
        fresh_rot, key_column_count + kv_head * HEAD_SIZE, HEAD_SIZE, 1
    )
    all_keys = jnp.concatenate(
        [arrived[:, :, :HEAD_SIZE].reshape(tp_size * slots_here, HEAD_SIZE), local_key_rows], axis=0
    )
    all_values = jnp.concatenate(
        [arrived[:, :, HEAD_SIZE:].reshape(tp_size * slots_here, HEAD_SIZE), local_value_rows],
        axis=0,
    )
    cache_mask = jnp.broadcast_to(
        (jnp.arange(tp_size * slots_here, dtype=jnp.int32) < cached_len)[None, :],
        (SPAN_TOKENS, tp_size * slots_here),
    )
    fresh_mask = token_index[None, :] <= token_index[:, None]
    visible_key_mask = jnp.concatenate([cache_mask, fresh_mask], axis=1)
    head_queries = queries.reshape(SPAN_TOKENS, heads_here, HEAD_SIZE)

    def per_query(head_slot):
        one_head = lax.dynamic_index_in_dim(head_queries, head_slot, 1, keepdims=False)
        scores = jnp.einsum(
            "td,kd->tk", one_head, all_keys, preferred_element_type=jnp.float32
        ) * HEAD_SIZE ** (-0.5)
        scores = jnp.where(visible_key_mask, scores, NEG_FILL)
        top_score = jnp.max(scores, axis=1, keepdims=True)
        weights = jnp.exp(scores - top_score)
        denominator = jnp.sum(weights, axis=1, keepdims=True)
        summed = jnp.dot(
            weights.astype(jnp.bfloat16), all_values, preferred_element_type=jnp.float32
        )
        return summed / denominator

    outputs = lax.map(per_query, jnp.arange(heads_here, dtype=jnp.int32))
    attended = (
        jnp.transpose(outputs, (1, 0, 2))
        .reshape(SPAN_TOKENS, heads_here * HEAD_SIZE)
        .astype(jnp.bfloat16)
    )
    out_weight = w_out[0]
    block_share = lax.psum_scatter(
        lax.dot_general(
            out_weight, attended, (((0,), (1,)), ((), ())), preferred_element_type=jnp.float32
        ).astype(jnp.bfloat16),
        "tp",
        scatter_dimension=0,
        tiled=True,
    ).astype(jnp.float32)
    updated = (own_rows.astype(jnp.float32) + block_share.T).astype(jnp.bfloat16)
    handed = passed_along(updated, "section", 1)
    return (handed[None], picked.reshape(1, 1, MOST, PAGE, 2 * key_column_count))


def solution(mesh):
    return jax.shard_map(
        on_device,
        mesh=mesh,
        in_specs=(
            P("section", "groups", "tp"),
            P("section", None),
            P("section", None, "tp"),
            P("section", None, "tp"),
            P("section", "tp", None),
            P("section", ("groups", "tp"), None),
            P("section", "groups"),
            P("section", "groups"),
        ),
        out_specs=(P("section", "groups", "tp"), P("section", "tp", "groups", None, None)),
        check_vma=False,
    )
```

profile of v0, /device:TPU:1, one launch (start us, length us, event | category | flops | bytes accessed | tf_op | source)
XLA Modules:
  0.0 357.5 jit_solution(11042912884622411416)
XLA Ops:
  7.2 6.4 %copy.41 = bf16[1,1024,2048]{1,2,0:T(8,128)(2,1)} copy(bf16[1,1024,2048]{2,1,0:T(8,128)(2,1)} %param.17) | data formatting | bytes 8388608 | tf_op args[5]
  13.6 6.2 %copy.42 = bf16[1024,2,8,128]{3,0,2,1:T(8,128)(2,1)} copy(bf16[1024,2,8,128]{0,3,2,1:T(8,128)(2,1)} %bitcast.83) | data formatting | bytes 8388608 | tf_op jit(solution)/shard_map/reshape;squeeze | solution.py:109
  19.8 5.2 %gather_fusion = bf16[8,1024,2,128]{3,1,2,0:T(8,128)(2,1)} fusion(bf16[1024,2,8,128]{3,0,2,1:T(8,128)(2,1)} %copy.42, s32[1024]{0:T(1024)S(1)} %pad_clamp_fusion), kind=kCustom, calls=%fused_computation | custom fusion | bytes 8388640 | tf_op jit(solution)/shard_map/gather | solution.py:109
  25.1 6.5 %copy.43 = bf16[8,1024,2,128]{1,3,2,0:T(8,128)(2,1)} copy(bf16[8,1024,2,128]{3,1,2,0:T(8,128)(2,1)} %gather_fusion) | data formatting | bytes 8388608 | tf_op jit(solution)/shard_map/gather | solution.py:109
  31.5 6.4 %all-to-all-start = ((bf16[8,1024,256]{1,2,0:T(8,128)(2,1)}), bf16[8,1024,256]{1,2,0:T(8,128)(2,1)}, u32[]{:S(2)}, u32[]{:S(2)}) async-start(bf16[8,1024,256]{1,2,0:T(8,128)(2,1)} %bitcast.82), calls=%async_computation | async-start | bytes 8388608 | tf_op jit(solution)/shard_map/all_to_all | solution.py:111
  38.7 21.0 %copy.50 = bf16[1024,8192]{1,0:T(8,128)(2,1)} copy(bf16[1024,8192]{0,1:T(8,128)(2,1)} %bitcast.80) | data formatting | bytes 33554432 | tf_op jit(solution)/shard_map/dot_general | solution.py:95
  60.9 83.6 %all-gather.3.cloned.1.call-done = bf16[1,128,8192]{2,1,0:T(8,128)(2,1)} async-done(((bf16[1,128,1024]{2,1,0:T(8,128)(2,1)}), bf16[1,128,8192]{2,1,0:T(8,128)(2,1)}) %all-gather.3.cloned.1.call-update) | async-done | bytes 2097168 | tf_op jit(solution)/shard_map/all_gather | solution.py:85
  144.5 2.1 fusion.23
  146.6 3.6 %fusion.30 = bf16[128,256]{1,0:T(8,128)(2,1)S(1)} fusion(bf16[1,8192,256]{2,1,0:T(8,128)(2,1)} %param.15, bf16[1,128,8192]{2,1,0:T(8,128)(2,1)} %all-gather.3.cloned.1.call-done, f32[8192]{0:T(1024)S(1)} %bitcast.92, f32[128]{0:T(128)S(1)} %add_rsqrt_fusion), kind=kOutput, calls=%fused_computation.31 | convolution fusion | flops 541097984 | bytes 6390272 | tf_op jit(solution)/shard_map/dot_general | solution.py:103
  150.2 26.0 %all_gather.7 = bf16[128,2048]{1,0:T(8,128)(2,1)S(1)} all-gather(bf16[128,256]{1,0:T(8,128)(2,1)S(1)} %fusion.30), channel_id=1, replica_groups=mesh['groups'=2,'section'=2,'tp'=8] {'tp'}, dimensions={1}, use_global_device_ids=true | all-gather | bytes 589824 | tf_op jit(solution)/shard_map/all_gather | solution.py:112
  176.5 8.8 %fusion.28 = f32[128,8,128]{0,2,1:T(8,128)S(1)} fusion(bf16[8,128,8192]{2,1,0:T(8,128)(2,1)} %bitcast.81, bf16[1,128,8192]{2,1,0:T(8,128)(2,1)} %all-gather.3.cloned.1.call-done, f32[8192]{0:T(1024)S(1)} %bitcast.93, f32[128]{0:T(128)S(1)} %add_rsqrt_fusion), kind=kOutput, calls=%fused_computation.29 | convolution fusion | flops 2151677952 | bytes 19431936 | tf_op jit(solution)/shard_map/dot_general | solution.py:95
  187.1 4.2 %fusion.44 = (bf16[8,1024,128]{1,2,0:T(8,128)(2,1)S(1)}, bf16[8,1024,128]{1,2,0:T(8,128)(2,1)}) fusion(bf16[8,1024,256]{1,2,0:T(8,128)(2,1)} %all-to-all-done), kind=kLoop, calls=%fused_computation.66 | loop fusion | bytes 8388608 | tf_op jit(solution)/shard_map/slice | solution.py:124
  191.3 3.9 %copy.44 = bf16[8,1024,128]{2,1,0:T(8,128)(2,1)} copy(bf16[8,1024,128]{1,2,0:T(8,128)(2,1)} %get-tuple-element.92) | data formatting | bytes 4194304 | tf_op jit(solution)/shard_map/slice | solution.py:121
  195.2 2.4 copy.47
  197.6 5.3 %pad_maximum_fusion = bf16[8320,128]{1,0:T(8,128)(2,1)S(1)} fusion(bf16[128,128]{1,0:T(8,128)(2,1)S(1)} %get-tuple-element.98, bf16[8192,128]{1,0:T(8,128)(2,1)} %bitcast.85), kind=kLoop, calls=%fused_computation.27 | loop fusion | flops 4259840 | bytes 4259840 | tf_op jit(solution)/shard_map/concatenate | solution.py:120
  202.9 5.0 %pad_maximum_fusion.1 = bf16[8320,128]{1,0:T(8,128)(2,1)} fusion(bf16[128,128]{1,0:T(8,128)(2,1)S(1)} %get-tuple-element.97, bf16[8192,128]{1,0:T(8,128)(2,1)S(1)} %bitcast.84), kind=kLoop, calls=%fused_computation.28 | loop fusion | flops 4259840 | bytes 4259840 | tf_op jit(solution)/shard_map/concatenate | solution.py:123
  207.9 56.9 %while.10 = (s32[]{:T(128)}, bf16[8,128,128]{1,2,0:T(8,128)(2,1)}, s32[8]{0:T(128)S(1)}, bf16[128,8,128]{0,2,1:T(8,128)(2,1)}, bf16[8320,128]{1,0:T(8,128)(2,1)S...) while((s32[]{:T(128)}, bf16[8,128,128]{1,2,0:T(8,128)(2,1)}, ...), condition=%wide.region_4.5_spmd, body=%wide.region_1.4_spmd.sunk | while | flops 552746752 | bytes 26823860 | solution.py:149
  217.7 2.0 fusion.60
  224.8 2.0 fusion.60
  231.9 2.0 fusion.60
  239.0 2.0 fusion.60
  264.8 9.7 %fusion.20 = bf16[8192,128]{0,1:T(8,128)(2,1)} fusion(bf16[128,1024]{0,1:T(8,128)(2,1)} %bitcast.89, bf16[1,1024,8192]{2,1,0:T(8,128)(2,1)} %param.16), kind=kOutput, calls=%fused_computation.18 | convolution fusion | flops 2148532224 | bytes 19136512 | tf_op jit(solution)/shard_map/dot_general | solution.py:157
  274.8 70.3 %reduce-scatter.2.cloned.1.call-done = bf16[1024,128]{0,1:T(8,128)(2,1)} async-done(((bf16[8192,128]{0,1:T(8,128)(2,1)}), bf16[1024,128]{0,1:T(8,128)(2,1)}) %reduce-scatter.2.cloned.1.call-update) | async-done | bytes 262160 | tf_op jit(solution)/shard_map/reduce_scatter | solution.py:156
  346.1 2.6 collective-permute-start
  (104 shorter events, 38.8 us)
Async XLA Ops:
  31.5 155.6 %all-to-all-start = ((bf16[8,1024,256]{1,2,0:T(8,128)(2,1)}), bf16[8,1024,256]{1,2,0:T(8,128)(2,1)}, u32[]{:S(2)}, u32[]{:S(2)}) async-start(bf16[8,1024,256]{1,2,0:T(8,128)(2,1)} %bitcast.82), calls=%async_computation | async-start | bytes 8388608 | tf_op jit(solution)/shard_map/all_to_all | solution.py:111
  37.9 106.6 %all-gather.3.cloned.1.call-start = ((), (), s32[]{:S(2)}) async-start(), calls=%async_computation.3 | async-start | bytes 2359296 | tf_op jit(solution)/shard_map/all_gather | solution.py:85
  38.6 306.4 %reduce-scatter.2.cloned.1.call-start = ((), (), s32[]{:S(2)}) async-start(), calls=%async_computation.2 | async-start | bytes 2359296 | tf_op jit(solution)/shard_map/reduce_scatter | solution.py:156
  38.7 107.9 %copy-start.5 = (f32[1,8192]{1,0:T(1,128)S(1)}, f32[1,8192]{1,0:T(1,128)}, u32[]{:S(2)}) copy-start(f32[1,8192]{1,0:T(1,128)} %param.13) | copy-start | bytes 98308
  186.4 0.7 copy-start.2
  197.6 5.3 %copy-start.1 = (bf16[8,1024,128]{2,1,0:T(8,128)(2,1)S(1)}, bf16[8,1024,128]{2,1,0:T(8,128)(2,1)}, u32[]{:S(2)}) copy-start(bf16[8,1024,128]{2,1,0:T(8,128)(2,1)} %copy.47) | copy-start | bytes 6291460
  210.6 2.8 copy-start
  217.7 2.8 copy-start
  224.8 2.8 copy-start
  231.9 2.8 copy-start
  239.0 2.8 copy-start
  246.1 2.8 copy-start
  253.3 2.8 copy-start
  260.4 2.8 copy-start
  264.8 9.8 %copy-start.6 = (s32[1,16]{1,0:T(1,128)S(1)}, s32[1,16]{1,0:T(1,128)}, u32[]{:S(2)}) copy-start(s32[1,16]{1,0:T(1,128)} %param.19) | copy-start | bytes 196
  264.8 80.3 %copy-start.4 = (bf16[1,128,1024]{2,1,0:T(8,128)(2,1)S(1)}, bf16[1,128,1024]{2,1,0:T(8,128)(2,1)}, u32[]{:S(2)}) copy-start(bf16[1,128,1024]{2,1,0:T(8,128)(2,1)} %param.12) | copy-start | bytes 786436
  264.8 83.9 %copy-start.3 = (bf16[128,1024]{1,0:T(8,128)(2,1)S(1)}, bf16[128,1024]{1,0:T(8,128)(2,1)}, u32[]{:S(2)}) copy-start(bf16[128,1024]{1,0:T(8,128)(2,1)} %copy-done.2) | copy-start | bytes 786436
  346.1 3.8 %collective-permute-start = (bf16[128,1024]{1,0:T(8,128)(2,1)S(1)}, bf16[128,1024]{1,0:T(8,128)(2,1)S(1)}, u32[]{:S(2)}, u32[]{:S(2)}) collective-permute-start(bf16[128,1024]{1,0:T(8,128)(2,1)S(1)} %fusion.35), channel_id=1, source_target_pairs={{0,8},{8,0},{1,9},{9,1},{2,10},{10,2},{3,11},{11,3},{4,12},{12,4},... | collective-permute-start | bytes 786440 | tf_op jit(solution)/shard_map/ppermute | solution.py:22
Sparse Core Ops, SparseCore 0:
  40.9 103.5 all-gather.2
  274.7 70.3 reduce-scatter.1
where the time goes:
time: 359 us; the launch traced here: 358 us
  waiting for transfers between devices  155 us (43%)
  local copies, waits for them, and re-layouts  69.6 us (19%)
  matrix products  45.3 us (13%)
  blocking collectives  26 us (7%)
  other arithmetic  21.5 us (6%)
  loops' own time  16.5 us (5%)
  between operations  14.9 us (4%)
  starting transfers between devices  9.05 us (3%)
    all_gather x1, waiting for transfers between devices, on_device(): full_rows = lax.all_gather(own_rows, 'tp', axis=1, tiled=True)  83.6 us
    reduce_scatter x1, waiting for transfers between devices, on_device(): lax.psum_scatter(lax.dot_general(out_weight, attended, (((0,), (1,)), (()...  70.3 us
    all_gather x1, blocking collectives, on_device(): fresh_all = lax.all_gather(fresh_part, 'tp', axis=1, tiled=True)  26 us
    dot_general x1, local copies, waits for them, and re-layouts, on_device(): jnp.dot(normed, w_query[0], preferred_element_type=jnp.float32)  21 us
    another operation x1, loops' own time, on_device(): outputs = lax.map(per_query, jnp.arange(heads_here, dtype=jnp.int32))  16.5 us
    dot_general x8, matrix products, per_query(): jnp.einsum('td,kd->tk', one_head, all_keys, preferred_element_type=jnp.fl...  16.1 us
    gather x2, local copies, waits for them, and re-layouts, on_device(): cached.reshape(slots_here, 2, KEY_VALUE_HEADS, HEAD_SIZE)  11.7 us
    dot_general x1, matrix products, on_device(): lax.dot_general(out_weight, attended, (((0,), (1,)), ((), ())), preferred...  9.72 us
  transfers between devices with their start and end apart: 4, of which 2 were waited for; matrix products, arithmetic and copies ran while one was open for 11% of the time, Pallas kernels for 0%

commit v1 on v0

--- a/solution.py
+++ b/solution.py
@@ -1,7 +1,11 @@
+import functools
+
 import jax
 import jax.numpy as jnp
 import numpy as np
 from jax import lax
+from jax.experimental import pallas as pl
+from jax.experimental.pallas import tpu as pltpu
 from jax.sharding import PartitionSpec as P
 
 QUERY_HEADS = 64
@@ -73,7 +77,7 @@
     return (picked, slot_page, slot_live)
 
 
-def on_device(
+def on_device_plain(
     hidden, norm_gain, w_query, key_value_weight, w_out, cache_pages, prefix_len, page_owner
 ):
     tp_size = lax.axis_size("tp")
@@ -106,8 +110,10 @@
     cached = cache_pages[0]
     slots_here = cached.shape[0]
     head_table = np.arange(tp_size) * heads_here // query_group_width
-    split_view = cached.reshape(slots_here, 2, KEY_VALUE_HEADS, HEAD_SIZE)[:, :, head_table, :]
-    outgoing = jnp.transpose(split_view, (2, 0, 1, 3)).reshape(tp_size, slots_here, 2 * HEAD_SIZE)
+    by_head = jnp.transpose(
+        cached.reshape(slots_here, 2, KEY_VALUE_HEADS, HEAD_SIZE), (2, 0, 1, 3)
+    ).reshape(KEY_VALUE_HEADS, slots_here, 2 * HEAD_SIZE)
+    outgoing = jnp.stack([by_head[int(h)] for h in head_table])
     arrived = lax.all_to_all(outgoing, "tp", split_axis=0, concat_axis=0, tiled=True)
     fresh_all = lax.all_gather(fresh_part, "tp", axis=1, tiled=True)
     fresh_rot = rotate_fresh(fresh_all, token_places)
@@ -164,6 +170,441 @@
     updated = (own_rows.astype(jnp.float32) + block_share.T).astype(jnp.bfloat16)
     handed = passed_along(updated, "section", 1)
     return (handed[None], picked.reshape(1, 1, MOST, PAGE, 2 * key_column_count))
+
+
+LOG2E = 1.4426950408889634
+VMEM_BYTES = 60 * 1024 * 1024
+ANY = pl.BlockSpec(memory_space=pl.ANY)
+VMEM = pl.BlockSpec(memory_space=pltpu.VMEM)
+
+
+def layer_kernel(
+    n, sections, heads_here,
+    own_ref, gain_ref, cos_ref, sin_ref, bias_ref, wq_hbm, wkv_hbm, wo_hbm, cache_hbm,
+    handed_ref, fresh_ref,
+    wq, wkv, wo, cache, vt, hbuf, acc, sumsq, qbuf, obuf, mlbuf, own_o, own_ml, kvbuf, att,
+    rbuf, upd, landed,
+    w_sem, h_send, h_recv, q_send, q_recv, kv_send, kv_recv, o_send, o_recv, ml_send, ml_recv,
+    r_send, r_recv, x_send, x_recv,
+):
+    f32, bf16 = jnp.float32, jnp.bfloat16
+    tokens, width = own_ref.shape
+    half = width // 2
+    half_heads = heads_here // 2
+    q_cols = heads_here * HEAD_SIZE
+    kv_cols = wkv.shape[1]
+    kv_half = kv_cols // 2
+    key_cols = KEY_VALUE_HEADS * HEAD_SIZE
+    rows = half_heads * tokens
+    group = QUERY_HEADS // KEY_VALUE_HEADS
+
+    me = lax.axis_index("tp")
+    z, y = lax.div(me, 2), lax.rem(me, 2)
+    place = y * (n - 1 - z) + (1 - y) * z
+
+    def at_place(p):
+        p = lax.rem(p + 2 * n, n)
+        c = lax.div(p, n // 2)
+        return (1 - c) * (2 * p) + c * (2 * (n - 1 - p) + 1)
+
+    to = (at_place(place + 1), at_place(place - 1))
+
+    def owner_at(d, s):
+        return at_place(place - s) if d == 0 else at_place(place + s)
+
+    def send(src, dst, ssem, rsem, d):
+        return pltpu.make_async_remote_copy(
+            src_ref=src, dst_ref=dst, send_sem=ssem, recv_sem=rsem,
+            device_id={"tp": to[d]}, device_id_type=pl.DeviceIdType.MESH,
+        )
+
+    loads = [
+        pltpu.make_async_copy(src, dst, w_sem.at[i])
+        for i, (src, dst) in enumerate(
+            ((wq_hbm, wq), (wkv_hbm, wkv), (cache_hbm, cache), (wo_hbm, wo))
+        )
+    ]
+    loads[0].start()
+    loads[1].start()
+
+    sec = lax.axis_index("section")
+    sec_next = lax.rem(sec + 1, sections)
+    sec_prev = lax.rem(sec + sections - 1, sections)
+    barrier = pltpu.get_barrier_semaphore()
+    for d in range(2):
+        pl.semaphore_signal(
+            barrier, inc=1, device_id={"tp": to[d]}, device_id_type=pl.DeviceIdType.MESH
+        )
+    pl.semaphore_signal(
+        barrier, inc=1, device_id={"section": sec_prev}, device_id_type=pl.DeviceIdType.MESH
+    )
+    for d in range(2):
+        hbuf[d, 0] = own_ref[:, d * half : (d + 1) * half]
+    acc[...] = jnp.zeros_like(acc)
+    sumsq[...] = jnp.zeros_like(sumsq)
+    pl.semaphore_wait(barrier, 3)
+
+    def h_copy(d, s):
+        return send(
+            hbuf.at[d, s], hbuf.at[d, s + 1], h_send.at[d, s], h_recv.at[d, s + 1], d
+        )
+
+    def h_arrival(d, s):
+        return send(hbuf.at[d, s - 1], hbuf.at[d, s], h_send.at[d, s], h_recv.at[d, s], d)
+
+    def project(s, carry):
+        for d in range(2):
+
+            @pl.when(s > 0)
+            def _():
+                h_arrival(d, s).wait_recv()
+
+            @pl.when(s < n - 1)
+            def _():
+                h_copy(d, s).start()
+
+        @pl.when(s == 0)
+        def _():
+            loads[0].wait()
+            loads[1].wait()
+            loads[2].start()
+            loads[3].start()
+
+        for d in range(2):
+            first = pl.multiple_of(owner_at(d, s) * width + d * half, 128)
+            part = hbuf[d, s].astype(f32)
+            sumsq[...] += jnp.sum(part * part, axis=1, keepdims=True)
+            scaled = (part * gain_ref[:, pl.ds(first, half)]).astype(bf16)
+            acc[:, :q_cols] += jnp.dot(
+                scaled, wq[pl.ds(first, half), :], preferred_element_type=f32
+            )
+            acc[:, q_cols:] += jnp.dot(
+                scaled, wkv[pl.ds(first, half), :], preferred_element_type=f32
+            )
+        return carry
+
+    lax.fori_loop(0, n, project, 0)
+
+    scale = lax.rsqrt(sumsq[...] * (1.0 / (width * n)) + 1e-05)
+    cosine, sine = cos_ref[...], sin_ref[...]
+
+    def rotary(v):
+        return v * cosine + pltpu.roll(v, HEAD_SIZE // 2, 1) * sine
+
+    for h in range(heads_here):
+        d, hh = h // half_heads, h % half_heads
+        v = acc[:, h * HEAD_SIZE : (h + 1) * HEAD_SIZE] * scale
+        qbuf[d, 0, hh * tokens : (hh + 1) * tokens, :] = rotary(v).astype(bf16)
+
+    def q_copy(d, s):
+        return send(
+            qbuf.at[d, s], qbuf.at[d, s + 1], q_send.at[d, s], q_recv.at[d, s + 1], d
+        )
+
+    def q_arrival(d, s):
+        return send(qbuf.at[d, s - 1], qbuf.at[d, s], q_send.at[d, s], q_recv.at[d, s], d)
+
+    def kv_copy(d, s):
+        return send(
+            kvbuf.at[d, s], kvbuf.at[d, s + 1], kv_send.at[d, s], kv_recv.at[d, s + 1], d
+        )
+
+    def kv_arrival(d, s):
+        return send(kvbuf.at[d, s - 1], kvbuf.at[d, s], kv_send.at[d, s], kv_recv.at[d, s], d)
+
+    def after(s):
+        return lax.rem(s + 1, n)
+
+    def o_copies(d, s):
+        t = after(s)
+        return (
+            send(obuf.at[d, s], obuf.at[d, t], o_send.at[d, s], o_recv.at[d, t], d),
+            send(mlbuf.at[d, s], mlbuf.at[d, t], ml_send.at[d, s], ml_recv.at[d, t], d),
+        )
+
+    def o_arrivals(d, t):
+        s = lax.rem(t + n - 1, n)
+        return (
+            send(obuf.at[d, s], obuf.at[d, t], o_send.at[d, s], o_recv.at[d, t], d),
+            send(mlbuf.at[d, s], mlbuf.at[d, t], ml_send.at[d, s], ml_recv.at[d, t], d),
+        )
+
+    for d in range(2):
+        q_copy(d, 0).start()
+    is_key = jnp.broadcast_to(me * kv_cols, (tokens, HEAD_SIZE)) < key_cols
+    for d in range(2):
+        for c in range(kv_half // HEAD_SIZE):
+            a = q_cols + d * kv_half + c * HEAD_SIZE
+            v = (acc[:, a : a + HEAD_SIZE] * scale).astype(bf16).astype(f32)
+            turned = jnp.where(is_key, rotary(v), v)
+            kvbuf[d, 0, :, c * HEAD_SIZE : (c + 1) * HEAD_SIZE] = turned.astype(bf16)
+        kv_copy(d, 0).start()
+
+    loads[2].wait()
+    for g in range(KEY_VALUE_HEADS):
+        a = key_cols + g * HEAD_SIZE
+        vt[g * HEAD_SIZE : (g + 1) * HEAD_SIZE, :] = cache[:, a : a + HEAD_SIZE].T
+
+    factor = HEAD_SIZE ** (-0.5) * LOG2E
+
+    def merged(m1, l1, o1, m2, l2, o2):
+        m = jnp.maximum(m1, m2)
+        a, b = jnp.exp2(m1 - m), jnp.exp2(m2 - m)
+        return m, l1 * a + l2 * b, o1 * a + o2 * b
+
+    def partial(keys, values_t, q, bias):
+        scores = lax.dot_general(
+            keys, q, (((1,), (1,)), ((), ())), preferred_element_type=f32
+        ) * factor + bias
+        m = jnp.max(scores, axis=0, keepdims=True)
+        p = jnp.exp2(scores - m)
+        l = jnp.sum(p, axis=0, keepdims=True)
+        o = jnp.dot(values_t, p.astype(bf16), preferred_element_type=f32)
+        return m, l, o
+
+    def attend(s, carry):
+        for d in range(2):
+
+            @pl.when(s > 0)
+            def _():
+                q_arrival(d, s).wait_recv()
+
+            @pl.when((s > 0) & (s < n - 1))
+            def _():
+                q_copy(d, s).start()
+
+        for d in range(2):
+
+            @pl.when(s > 0)
+            def _():
+                kv_arrival(d, s).wait_recv()
+
+            @pl.when((s > 0) & (s < n - 1))
+            def _():
+                kv_copy(d, s).start()
+
+            owner = owner_at(d, s)
+            col = pl.multiple_of(owner * kv_cols + d * kv_half, 128)
+            fresh_ref[:, pl.ds(col, kv_half)] = kvbuf[d, s]
+
+        for d in range(2):
+            owner = owner_at(d, s)
+            head = lax.div(owner * heads_here, group)
+            first = pl.multiple_of(head * HEAD_SIZE, HEAD_SIZE)
+            keys = cache[:, pl.ds(first, HEAD_SIZE)]
+            values_t = vt[pl.ds(first, HEAD_SIZE), :]
+            bias = bias_ref[...]
+            parts = [
+                partial(keys, values_t, qbuf[d, s, r : r + tokens, :], bias)
+                for r in range(0, rows, tokens)
+            ]
+
+            @pl.when(s > 1)
+            def _():
+                for c in o_arrivals(d, s):
+                    c.wait_recv()
+
+            for i, (m, l, o) in enumerate(parts):
+                span = slice(i * tokens, (i + 1) * tokens)
+
+                @pl.when(s == 0)
+                def _():
+                    own_o[d, :, span] = o
+                    own_ml[d, 0:1, span] = m
+                    own_ml[d, 1:2, span] = l
+
+                @pl.when(s == 1)
+                def _():
+                    obuf[d, s, :, span] = o.astype(bf16)
+                    mlbuf[d, s, 0:1, span] = m
+                    mlbuf[d, s, 1:2, span] = l
+                    mlbuf[d, s, 2:8, span] = jnp.zeros((6, tokens), f32)
+
+                @pl.when(s > 1)
+                def _():
+                    m3, l3, o3 = merged(
+                        mlbuf[d, s, 0:1, span], mlbuf[d, s, 1:2, span],
+                        obuf[d, s, :, span].astype(f32), m, l, o,
+                    )
+                    obuf[d, s, :, span] = o3.astype(bf16)
+                    mlbuf[d, s, 0:1, span] = m3
+                    mlbuf[d, s, 1:2, span] = l3
+
+            @pl.when(s > 0)
+            def _():
+                for c in o_copies(d, s):
+                    c.start()
+
+        return carry
+
+    lax.fori_loop(0, n, attend, 0)
+
+    head = lax.div(me * heads_here, group)
+    first = pl.multiple_of(head * HEAD_SIZE, HEAD_SIZE)
+    fresh_keys = fresh_ref[:, pl.ds(first, HEAD_SIZE)]
+    fresh_values_t = fresh_ref[
+        :, pl.ds(pl.multiple_of(first + key_cols, HEAD_SIZE), HEAD_SIZE)
+    ].T
+    key_at = lax.broadcasted_iota(jnp.int32, (tokens, tokens), 0)
+    query_at = lax.broadcasted_iota(jnp.int32, (tokens, tokens), 1)
+    causal = jnp.where(key_at <= query_at, 0.0, NEG_FILL)
+    for d in range(2):
+        own_parts = []
+        for i in range(half_heads):
+            span = slice(i * tokens, (i + 1) * tokens)
+            m, l, o = partial(fresh_keys, fresh_values_t, qbuf[d, 0, span, :], causal)
+            own_parts.append(
+                merged(own_ml[d, 0:1, span], own_ml[d, 1:2, span], own_o[d, :, span], m, l, o)
+            )
+        for c in o_arrivals(d, 0):
+            c.wait_recv()
+        for i in range(half_heads):
+            span = slice(i * tokens, (i + 1) * tokens)
+            _, l, o = merged(
+                mlbuf[d, 0, 0:1, span], mlbuf[d, 0, 1:2, span],
+                obuf[d, 0, :, span].astype(f32), *own_parts[i],
+            )
+            h = d * half_heads + i
+            att[:, h * HEAD_SIZE : (h + 1) * HEAD_SIZE] = (o / l).T.astype(bf16)
+
+    loads[3].wait()
+
+    def r_copy(d, s):
+        t = after(s)
+        return send(rbuf.at[d, s], rbuf.at[d, t], r_send.at[d, s], r_recv.at[d, t], d)
+
+    def r_arrival(d, t):
+        s = lax.rem(t + n - 1, n)
+        return send(rbuf.at[d, s], rbuf.at[d, t], r_send.at[d, s], r_recv.at[d, t], d)
+
+    def share(d, owner):
+        col = pl.multiple_of(owner * width + d * half, 128)
+        return jnp.dot(att[...], wo[:, pl.ds(col, half)], preferred_element_type=f32)
+
+    def scatter(s, carry):
+        for d in range(2):
+            part = share(d, owner_at(d, s))
+
+            @pl.when(s > 1)
+            def _():
+                r_arrival(d, s).wait_recv()
+                rbuf[d, s] = (rbuf[d, s].astype(f32) + part).astype(bf16)
+
+            @pl.when(s == 1)
+            def _():
+                rbuf[d, s] = part.astype(bf16)
+
+            r_copy(d, s).start()
+        return carry
+
+    lax.fori_loop(1, n, scatter, 0)
+
+    def cross(d):
+        return pltpu.make_async_remote_copy(
+            src_ref=upd.at[d], dst_ref=landed.at[d], send_sem=x_send.at[d],
+            recv_sem=x_recv.at[d], device_id={"section": sec_next},
+            device_id_type=pl.DeviceIdType.MESH,
+        )
+
+    mine = [own_ref[:, d * half : (d + 1) * half].astype(f32) + share(d, me) for d in range(2)]
+    for d in range(2):
+        r_arrival(d, 0).wait_recv()
+        upd[d] = (mine[d] + rbuf[d, 0].astype(f32)).astype(bf16)
+        cross(d).start()
+    for d in range(2):
+        cross(d).wait_recv()
+        handed_ref[:, d * half : (d + 1) * half] = landed[d]
+
+    def sent(s, carry):
+        for d in range(2):
+            h_copy(d, s).wait_send()
+            q_copy(d, s).wait_send()
+            kv_copy(d, s).wait_send()
+            for c in o_copies(d, s + 1):
+                c.wait_send()
+            r_copy(d, s + 1).wait_send()
+        return carry
+
+    lax.fori_loop(0, n - 1, sent, 0)
+    for d in range(2):
+        cross(d).wait_send()
+
+
+def on_device(
+    hidden, norm_gain, w_query, key_value_weight, w_out, cache_pages, prefix_len, page_owner
+):
+    n = lax.axis_size("tp")
+    heads_here = QUERY_HEADS // n
+    tokens, width = hidden.shape[1:]
+    kv_cols = key_value_weight.shape[2]
+    if heads_here % 2 or kv_cols % (2 * HEAD_SIZE) or n % 2 or width % 256:
+        return on_device_plain(
+            hidden, norm_gain, w_query, key_value_weight, w_out, cache_pages, prefix_len,
+            page_owner,
+        )
+    sections = lax.axis_size("section")
+    me = lax.axis_index("tp")
+    slots = cache_pages.shape[1]
+    half, half_heads = width // 2, heads_here // 2
+    rows = half_heads * tokens
+    cached_len = prefix_len[0, 0]
+    half_head = HEAD_SIZE // 2
+    inv_freq = ROPE_BASE ** (-jnp.arange(half_head, dtype=jnp.float32) * (2.0 / HEAD_SIZE))
+    places = (cached_len + jnp.arange(tokens, dtype=jnp.int32)).astype(jnp.float32)
+    angles = places[:, None] * inv_freq[None, :]
+    cosine, sine = jnp.cos(angles), jnp.sin(angles)
+    cos2 = jnp.concatenate([cosine, cosine], axis=1)
+    sin2 = jnp.concatenate([-sine, sine], axis=1)
+    slot_at = me * slots + jnp.arange(slots, dtype=jnp.int32)
+    bias = jnp.broadcast_to(
+        jnp.where(slot_at < cached_len, 0.0, NEG_FILL).astype(jnp.float32)[:, None],
+        (slots, tokens),
+    )
+    bf16, f32 = jnp.bfloat16, jnp.float32
+    q_cols = heads_here * HEAD_SIZE
+    full = norm_gain.shape[1]
+    kv_all = kv_cols * n
+    dma = pltpu.SemaphoreType.DMA
+    handed, fresh_rot = pl.pallas_call(
+        functools.partial(layer_kernel, n, sections, heads_here),
+        out_shape=(
+            jax.ShapeDtypeStruct((tokens, width), bf16),
+            jax.ShapeDtypeStruct((tokens, kv_all), bf16),
+        ),
+        in_specs=[VMEM] * 5 + [ANY] * 4,
+        out_specs=(VMEM, VMEM),
+        scratch_shapes=[
+            pltpu.VMEM((full, q_cols), bf16),
+            pltpu.VMEM((full, kv_cols), bf16),
+            pltpu.VMEM((q_cols, full), bf16),
+            pltpu.VMEM((slots, kv_all), bf16),
+            pltpu.VMEM((kv_all // 2, slots), bf16),
+            pltpu.VMEM((2, n, tokens, half), bf16),
+            pltpu.VMEM((tokens, q_cols + kv_cols), f32),
+            pltpu.VMEM((tokens, 1), f32),
+            pltpu.VMEM((2, n, rows, HEAD_SIZE), bf16),
+            pltpu.VMEM((2, n, HEAD_SIZE, rows), bf16),
+            pltpu.VMEM((2, n, 8, rows), f32),
+            pltpu.VMEM((2, HEAD_SIZE, rows), f32),
+            pltpu.VMEM((2, 8, rows), f32),
+            pltpu.VMEM((2, n, tokens, kv_cols // 2), bf16),
+            pltpu.VMEM((tokens, q_cols), bf16),
+            pltpu.VMEM((2, n, tokens, half), bf16),
+            pltpu.VMEM((2, tokens, half), bf16),
+            pltpu.VMEM((2, tokens, half), bf16),
+            dma((4,)),
+        ]
+        + [dma((2, n))] * 12
+        + [dma((2,))] * 2,
+        compiler_params=pltpu.CompilerParams(
+            collective_id=0, has_side_effects=True, vmem_limit_bytes=VMEM_BYTES
+        ),
+    )(
+        hidden[0], norm_gain, cos2, sin2, bias, w_query[0], key_value_weight[0], w_out[0],
+        cache_pages[0],
+    )
+    picked, _, _ = fresh_pages(fresh_rot, page_owner[0], me)
+    return (handed[None], picked.reshape(1, 1, MOST, PAGE, kv_all))
 
 
 def solution(mesh):

time: 359 us -> 135 us (0.38)
  waiting for transfers between devices: 155 us -> 0 us
  Pallas kernels: 0 us -> 126 us
  local copies, waits for them, and re-layouts: 69.6 us -> 4.68 us
  matrix products: 45.3 us -> 0.22 us
  blocking collectives: 26 us -> 0 us
  other arithmetic: 21.5 us -> 1.28 us
  loops' own time: 16.5 us -> 0 us
  between operations: 14.9 us -> 1.32 us
  starting transfers between devices: 9.05 us -> 0 us
    pallas_call x0 -> x1, Pallas kernels: none -> 126 us  [on_device(): pl.pallas_call(functools.partial(layer_kernel, n, sections, heads_here),...]
    all_gather x1 -> x0, waiting for transfers between devices: 83.6 us -> none  [on_device(): full_rows = lax.all_gather(own_rows, 'tp', axis=1, tiled=True)]
    reduce_scatter x1 -> x0, waiting for transfers between devices: 70.3 us -> none  [on_device(): lax.psum_scatter(lax.dot_general(out_weight, attended, (((0,), (1,)), (()...]
    dot_general x19 -> x0, matrix products: 45.1 us -> none  [the longest x8 16.1 us: per_query(): jnp.einsum('td,kd->tk', one_head, all_keys, preferred_element_type=jnp.fl...]
    all_gather x1 -> x0, blocking collectives: 26 us -> none  [on_device(): fresh_all = lax.all_gather(fresh_part, 'tp', axis=1, tiled=True)]
    dot_general x1 -> x0, local copies, waits for them, and re-layouts: 21 us -> none  [on_device(): jnp.dot(normed, w_query[0], preferred_element_type=jnp.float32)]
    another operation x1 -> x0, loops' own time: 16.5 us -> none  [on_device(): outputs = lax.map(per_query, jnp.arange(heads_here, dtype=jnp.int32))]
    gather x2 -> x0, local copies, waits for them, and re-layouts: 11.7 us -> none  [on_device(): cached.reshape(slots_here, 2, KEY_VALUE_HEADS, HEAD_SIZE)]
  transfers between devices with their start and end apart: 4 -> 0, of which waited for: 2 -> 0; matrix products, arithmetic and copies ran while one was open for 11% -> 0% of each run, Pallas kernels for 0% -> 0%
where the time goes in v1:
time: 135 us; the launch traced here: 134 us
  Pallas kernels  126 us (93%)
  local copies, waits for them, and re-layouts  4.68 us (3%)
    pallas_call x1, Pallas kernels, on_device(): pl.pallas_call(functools.partial(layer_kernel, n, sections, heads_here),...  126 us

profile of v1, /device:TPU:1, one launch (start us, length us, event | category | flops | bytes accessed | tf_op | source)
XLA Modules:
  0.0 133.7 jit_solution(9965960583912780281)
XLA Ops:
  1.3 0.3 fusion
  1.6 0.8 pad_maximum_fusion
  2.4 1.0 broadcast_in_dim.14.bias_ref
  3.4 0.0 copy-start
  3.4 126.2 %shard_map.95 = (bf16[128,1024]{1,0:T(8,128)(2,1)}, bf16[128,2048]{1,0:T(8,128)(2,1)}) custom-call(bf16[128,1024]{1,0:T(8,128)(2,1)} %bitcast.23, f32[1,8192]{1,0:T(1,128)} %gain_ref.1, f32[128,128]{1,0:T(8,128)} %get-tuple-element.9.cos_ref, f32[128,128]{1,0:T(8,128)} %get-tuple-element.10.sin_ref, f32[1024,128]{1,0:T(8,128)} %broadcast_in_dim.14.bias_ref, ...), custom_call_target="tpu_custom_call" | custom-call | tf_op jit(solution)/shard_map/pallas_call | solution.py:568
  129.6 1.3 reshape.29
  130.9 0.0 copy-done
  130.9 0.2 convert_reduce_fusion
  131.1 0.2 convolution_convert_fusion
  131.3 0.7 copy.12
  132.1 1.7 %copy.15 = bf16[1,128,1024]{2,1,0:T(8,128)(2,1)} copy(bf16[1,128,1024]{2,1,0:T(8,128)(2,1)} %bitcast.24) | data formatting | bytes 524288
  (4 shorter events, 0.0 us)
Async XLA Ops:
  3.4 127.5 %copy-start = (s32[1,16]{1,0:T(1,128)S(1)}, s32[1,16]{1,0:T(1,128)}, u32[]{:S(2)}) copy-start(s32[1,16]{1,0:T(1,128)} %param.15) | copy-start | bytes 196

commit v2 on v1

--- a/solution.py
+++ b/solution.py
@@ -184,8 +184,8 @@
     handed_ref, fresh_ref,
     wq, wkv, wo, cache, vt, hbuf, acc, sumsq, qbuf, obuf, mlbuf, own_o, own_ml, kvbuf, att,
     rbuf, upd, landed,
-    w_sem, h_send, h_recv, q_send, q_recv, kv_send, kv_recv, o_send, o_recv, ml_send, ml_recv,
-    r_send, r_recv, x_send, x_recv,
+    w_sem, q_send, q_recv, kv_send, kv_recv, o_send, o_recv, ml_send, ml_recv,
+    h_send, h_recv, r_send, r_recv, x_send, x_recv,
 ):
     f32, bf16 = jnp.float32, jnp.bfloat16
     tokens, width = own_ref.shape
@@ -244,24 +244,48 @@
     sumsq[...] = jnp.zeros_like(sumsq)
     pl.semaphore_wait(barrier, 3)
 
-    def h_copy(d, s):
+    piece = tokens // 2
+
+    def h_copy(d, s, c):
+        span = pl.ds(c * piece, piece)
         return send(
-            hbuf.at[d, s], hbuf.at[d, s + 1], h_send.at[d, s], h_recv.at[d, s + 1], d
-        )
-
-    def h_arrival(d, s):
-        return send(hbuf.at[d, s - 1], hbuf.at[d, s], h_send.at[d, s], h_recv.at[d, s], d)
+            hbuf.at[d, s, span], hbuf.at[d, s + 1, span],
+            h_send.at[d, s, c], h_recv.at[d, s + 1, c], d,
+        )
+
+    def h_arrival(d, s, c):
+        span = pl.ds(c * piece, piece)
+        return send(
+            hbuf.at[d, s - 1, span], hbuf.at[d, s, span],
+            h_send.at[d, s, c], h_recv.at[d, s, c], d,
+        )
+
+    turns = n // 2
+    turn_heads = KEY_VALUE_HEADS // turns
 
     def project(s, carry):
-        for d in range(2):
-
-            @pl.when(s > 0)
-            def _():
-                h_arrival(d, s).wait_recv()
-
-            @pl.when(s < n - 1)
-            def _():
-                h_copy(d, s).start()
+        for c in range(2):
+            for d in range(2):
+
+                @pl.when(s > 0)
+                def _():
+                    h_arrival(d, s, c).wait_recv()
+
+                @pl.when(s < n - 1)
+                def _():
+                    h_copy(d, s, c).start()
+
+        @pl.when(s == n - turns)
+        def _():
+            loads[2].wait()
+
+        @pl.when(s >= n - turns)
+        def _():
+            for k in range(turn_heads):
+                g = (s - (n - turns)) * turn_heads + k
+                a = pl.multiple_of(g * HEAD_SIZE, HEAD_SIZE)
+                b = pl.multiple_of(g * HEAD_SIZE + key_cols, HEAD_SIZE)
+                vt[pl.ds(a, HEAD_SIZE), :] = cache[:, pl.ds(b, HEAD_SIZE)].T
 
         @pl.when(s == 0)
         def _():
@@ -340,11 +364,6 @@
             kvbuf[d, 0, :, c * HEAD_SIZE : (c + 1) * HEAD_SIZE] = turned.astype(bf16)
         kv_copy(d, 0).start()
 
-    loads[2].wait()
-    for g in range(KEY_VALUE_HEADS):
-        a = key_cols + g * HEAD_SIZE
-        vt[g * HEAD_SIZE : (g + 1) * HEAD_SIZE, :] = cache[:, a : a + HEAD_SIZE].T
-
     factor = HEAD_SIZE ** (-0.5) * LOG2E
 
     def merged(m1, l1, o1, m2, l2, o2):
@@ -418,7 +437,6 @@
                     obuf[d, s, :, span] = o.astype(bf16)
                     mlbuf[d, s, 0:1, span] = m
                     mlbuf[d, s, 1:2, span] = l
-                    mlbuf[d, s, 2:8, span] = jnp.zeros((6, tokens), f32)
 
                 @pl.when(s > 1)
                 def _():
@@ -469,32 +487,38 @@
 
     loads[3].wait()
 
-    def r_copy(d, s):
-        t = after(s)
-        return send(rbuf.at[d, s], rbuf.at[d, t], r_send.at[d, s], r_recv.at[d, t], d)
-
-    def r_arrival(d, t):
-        s = lax.rem(t + n - 1, n)
-        return send(rbuf.at[d, s], rbuf.at[d, t], r_send.at[d, s], r_recv.at[d, t], d)
+    def r_between(d, s, t, c):
+        span = pl.ds(c * piece, piece)
+        return send(
+            rbuf.at[d, s, span], rbuf.at[d, t, span], r_send.at[d, s, c], r_recv.at[d, t, c], d
+        )
+
+    def r_copy(d, s, c):
+        return r_between(d, s, after(s), c)
+
+    def r_arrival(d, t, c):
+        return r_between(d, lax.rem(t + n - 1, n), t, c)
 
     def share(d, owner):
         col = pl.multiple_of(owner * width + d * half, 128)
         return jnp.dot(att[...], wo[:, pl.ds(col, half)], preferred_element_type=f32)
 
     def scatter(s, carry):
-        for d in range(2):
-            part = share(d, owner_at(d, s))
-
-            @pl.when(s > 1)
-            def _():
-                r_arrival(d, s).wait_recv()
-                rbuf[d, s] = (rbuf[d, s].astype(f32) + part).astype(bf16)
-
-            @pl.when(s == 1)
-            def _():
-                rbuf[d, s] = part.astype(bf16)
-
-            r_copy(d, s).start()
+        parts = [share(d, owner_at(d, s)) for d in range(2)]
+        for c in range(2):
+            span = slice(c * piece, (c + 1) * piece)
+            for d in range(2):
+
+                @pl.when(s > 1)
+                def _():
+                    r_arrival(d, s, c).wait_recv()
+                    rbuf[d, s, span] = (rbuf[d, s, span].astype(f32) + parts[d][span]).astype(bf16)
+
+                @pl.when(s == 1)
+                def _():
+                    rbuf[d, s, span] = parts[d][span].astype(bf16)
+
+                r_copy(d, s, c).start()
         return carry
 
     lax.fori_loop(1, n, scatter, 0)
@@ -508,7 +532,8 @@
 
     mine = [own_ref[:, d * half : (d + 1) * half].astype(f32) + share(d, me) for d in range(2)]
     for d in range(2):
-        r_arrival(d, 0).wait_recv()
+        for c in range(2):
+            r_arrival(d, 0, c).wait_recv()
         upd[d] = (mine[d] + rbuf[d, 0].astype(f32)).astype(bf16)
         cross(d).start()
     for d in range(2):
@@ -517,12 +542,13 @@
 
     def sent(s, carry):
         for d in range(2):
-            h_copy(d, s).wait_send()
+            for c in range(2):
+                h_copy(d, s, c).wait_send()
+                r_copy(d, s + 1, c).wait_send()
             q_copy(d, s).wait_send()
             kv_copy(d, s).wait_send()
             for c in o_copies(d, s + 1):
                 c.wait_send()
-            r_copy(d, s + 1).wait_send()
         return carry
 
     lax.fori_loop(0, n - 1, sent, 0)
@@ -537,7 +563,7 @@
     heads_here = QUERY_HEADS // n
     tokens, width = hidden.shape[1:]
     kv_cols = key_value_weight.shape[2]
-    if heads_here % 2 or kv_cols % (2 * HEAD_SIZE) or n % 2 or width % 256:
+    if heads_here % 2 or kv_cols % (2 * HEAD_SIZE) or KEY_VALUE_HEADS % (n // 2) or n % 2 or tokens % 32 or width % 256:
         return on_device_plain(
             hidden, norm_gain, w_query, key_value_weight, w_out, cache_pages, prefix_len,
             page_owner,
@@ -584,7 +610,7 @@
             pltpu.VMEM((tokens, 1), f32),
             pltpu.VMEM((2, n, rows, HEAD_SIZE), bf16),
             pltpu.VMEM((2, n, HEAD_SIZE, rows), bf16),
-            pltpu.VMEM((2, n, 8, rows), f32),
+            pltpu.VMEM((2, n, 2, rows), f32),
             pltpu.VMEM((2, HEAD_SIZE, rows), f32),
             pltpu.VMEM((2, 8, rows), f32),
             pltpu.VMEM((2, n, tokens, kv_cols // 2), bf16),
@@ -594,7 +620,8 @@
             pltpu.VMEM((2, tokens, half), bf16),
             dma((4,)),
         ]
-        + [dma((2, n))] * 12
+        + [dma((2, n))] * 8
+        + [dma((2, n, 2))] * 4
         + [dma((2,))] * 2,
         compiler_params=pltpu.CompilerParams(
             collective_id=0, has_side_effects=True, vmem_limit_bytes=VMEM_BYTES

time: 135 us -> 126 us (0.933)
  Pallas kernels: 126 us -> 118 us
    pallas_call x1, Pallas kernels: 126 us -> 118 us  [on_device(): pl.pallas_call(functools.partial(layer_kernel, n, sections, heads_here),...]
where the time goes in v2:
time: 126 us
  Pallas kernels  118 us (94%)
  local copies, waits for them, and re-layouts  4.68 us (4%)
  between operations  1.32 us (1%)
  other arithmetic  1.28 us (1%)
    pallas_call x1, Pallas kernels, on_device(): pl.pallas_call(functools.partial(layer_kernel, n, sections, heads_here),...  118 us

profile of v2, /device:TPU:1, one launch (start us, length us, event | category | flops | bytes accessed | tf_op | source)
XLA Modules:
  0.0 125.6 jit_solution(11316722993973227044)
XLA Ops:
  1.3 0.3 fusion
  1.6 0.8 pad_maximum_fusion
  2.4 1.0 broadcast_in_dim.14.bias_ref
  3.4 0.0 copy-start
  3.4 118.1 %shard_map.95 = (bf16[128,1024]{1,0:T(8,128)(2,1)}, bf16[128,2048]{1,0:T(8,128)(2,1)}) custom-call(bf16[128,1024]{1,0:T(8,128)(2,1)} %bitcast.23, f32[1,8192]{1,0:T(1,128)} %gain_ref.1, f32[128,128]{1,0:T(8,128)} %get-tuple-element.9.cos_ref, f32[128,128]{1,0:T(8,128)} %get-tuple-element.10.sin_ref, f32[1024,128]{1,0:T(8,128)} %broadcast_in_dim.14.bias_ref, ...), custom_call_target="tpu_custom_call" | custom-call | tf_op jit(solution)/shard_map/pallas_call | solution.py:594
  121.5 1.3 %reshape.29 = bf16[16,16384]{1,0:T(8,128)(2,1)S(1)} reshape(bf16[128,2048]{1,0:T(8,128)(2,1)} %get-tuple-element.5) | data formatting | bytes 1048576 | tf_op jit(solution)/shard_map/reshape | solution.py:71
  122.7 0.0 copy-done
  122.8 0.2 convert_reduce_fusion
  123.0 0.2 convolution_convert_fusion
  123.2 0.7 copy.12
  123.9 1.7 %copy.15 = bf16[1,128,1024]{2,1,0:T(8,128)(2,1)} copy(bf16[1,128,1024]{2,1,0:T(8,128)(2,1)} %bitcast.24) | data formatting | bytes 524288
  (4 shorter events, 0.0 us)
Async XLA Ops:
  3.4 119.4 %copy-start = (s32[1,16]{1,0:T(1,128)S(1)}, s32[1,16]{1,0:T(1,128)}, u32[]{:S(2)}) copy-start(s32[1,16]{1,0:T(1,128)} %param.15) | copy-start | bytes 196

commit v3 on v2

--- a/solution.py
+++ b/solution.py
@@ -184,8 +184,8 @@
     handed_ref, fresh_ref,
     wq, wkv, wo, cache, vt, hbuf, acc, sumsq, qbuf, obuf, mlbuf, own_o, own_ml, kvbuf, att,
     rbuf, upd, landed,
-    w_sem, q_send, q_recv, kv_send, kv_recv, o_send, o_recv, ml_send, ml_recv,
-    h_send, h_recv, r_send, r_recv, x_send, x_recv,
+    w_sem, q_send, q_recv, kv_send, kv_recv,
+    o_send, o_recv, ml_send, ml_recv, h_send, h_recv, r_send, r_recv, x_send, x_recv,
 ):
     f32, bf16 = jnp.float32, jnp.bfloat16
     tokens, width = own_ref.shape
@@ -339,19 +339,21 @@
     def after(s):
         return lax.rem(s + 1, n)
 
-    def o_copies(d, s):
-        t = after(s)
+    def o_between(d, s, t, c):
         return (
-            send(obuf.at[d, s], obuf.at[d, t], o_send.at[d, s], o_recv.at[d, t], d),
-            send(mlbuf.at[d, s], mlbuf.at[d, t], ml_send.at[d, s], ml_recv.at[d, t], d),
-        )
-
-    def o_arrivals(d, t):
-        s = lax.rem(t + n - 1, n)
-        return (
-            send(obuf.at[d, s], obuf.at[d, t], o_send.at[d, s], o_recv.at[d, t], d),
-            send(mlbuf.at[d, s], mlbuf.at[d, t], ml_send.at[d, s], ml_recv.at[d, t], d),
-        )
+            send(obuf.at[d, s, c], obuf.at[d, t, c], o_send.at[d, s, c], o_recv.at[d, t, c], d),
+            send(
+                mlbuf.at[d, s, c], mlbuf.at[d, t, c], ml_send.at[d, s, c], ml_recv.at[d, t, c], d
+            ),
+        )
+
+    def o_copies(d, s, c):
+        return o_between(d, s, after(s), c)
+
+    def o_arrivals(d, t, c):
+        return o_between(d, lax.rem(t + n - 1, n), t, c)
+
+    chunk = half_heads // 2
 
     for d in range(2):
         q_copy(d, 0).start()
@@ -406,6 +408,7 @@
             col = pl.multiple_of(owner * kv_cols + d * kv_half, 128)
             fresh_ref[:, pl.ds(col, kv_half)] = kvbuf[d, s]
 
+        parts = []
         for d in range(2):
             owner = owner_at(d, s)
             head = lax.div(owner * heads_here, group)
@@ -413,45 +416,53 @@
             keys = cache[:, pl.ds(first, HEAD_SIZE)]
             values_t = vt[pl.ds(first, HEAD_SIZE), :]
             bias = bias_ref[...]
-            parts = [
-                partial(keys, values_t, qbuf[d, s, r : r + tokens, :], bias)
-                for r in range(0, rows, tokens)
-            ]
-
-            @pl.when(s > 1)
-            def _():
-                for c in o_arrivals(d, s):
-                    c.wait_recv()
-
-            for i, (m, l, o) in enumerate(parts):
-                span = slice(i * tokens, (i + 1) * tokens)
-
-                @pl.when(s == 0)
-                def _():
-                    own_o[d, :, span] = o
-                    own_ml[d, 0:1, span] = m
-                    own_ml[d, 1:2, span] = l
-
-                @pl.when(s == 1)
-                def _():
-                    obuf[d, s, :, span] = o.astype(bf16)
-                    mlbuf[d, s, 0:1, span] = m
-                    mlbuf[d, s, 1:2, span] = l
+            parts.append(
+                [
+                    partial(keys, values_t, qbuf[d, s, r : r + tokens, :], bias)
+                    for r in range(0, rows, tokens)
+                ]
+            )
+
+        for c in range(2):
+            for d in range(2):
 
                 @pl.when(s > 1)
                 def _():
-                    m3, l3, o3 = merged(
-                        mlbuf[d, s, 0:1, span], mlbuf[d, s, 1:2, span],
-                        obuf[d, s, :, span].astype(f32), m, l, o,
-                    )
-                    obuf[d, s, :, span] = o3.astype(bf16)
-                    mlbuf[d, s, 0:1, span] = m3
-                    mlbuf[d, s, 1:2, span] = l3
-
-            @pl.when(s > 0)
-            def _():
-                for c in o_copies(d, s):
-                    c.start()
+                    for copy in o_arrivals(d, s, c):
+                        copy.wait_recv()
+
+                for k in range(chunk):
+                    i = c * chunk + k
+                    m, l, o = parts[d][i]
+                    own_span = slice(i * tokens, (i + 1) * tokens)
+                    span = slice(k * tokens, (k + 1) * tokens)
+
+                    @pl.when(s == 0)
+                    def _():
+                        own_o[d, :, own_span] = o
+                        own_ml[d, 0:1, own_span] = m
+                        own_ml[d, 1:2, own_span] = l
+
+                    @pl.when(s == 1)
+                    def _():
+                        obuf[d, s, c, :, span] = o.astype(bf16)
+                        mlbuf[d, s, c, 0:1, span] = m
+                        mlbuf[d, s, c, 1:2, span] = l
+
+                    @pl.when(s > 1)
+                    def _():
+                        m3, l3, o3 = merged(
+                            mlbuf[d, s, c, 0:1, span], mlbuf[d, s, c, 1:2, span],
+                            obuf[d, s, c, :, span].astype(f32), m, l, o,
+                        )
+                        obuf[d, s, c, :, span] = o3.astype(bf16)
+                        mlbuf[d, s, c, 0:1, span] = m3
+                        mlbuf[d, s, c, 1:2, span] = l3
+
+                @pl.when(s > 0)
+                def _():
+                    for copy in o_copies(d, s, c):
+                        copy.start()
 
         return carry
 
@@ -474,13 +485,15 @@
             own_parts.append(
                 merged(own_ml[d, 0:1, span], own_ml[d, 1:2, span], own_o[d, :, span], m, l, o)
             )
-        for c in o_arrivals(d, 0):
-            c.wait_recv()
+        for c in range(2):
+            for copy in o_arrivals(d, 0, c):
+                copy.wait_recv()
         for i in range(half_heads):
-            span = slice(i * tokens, (i + 1) * tokens)
+            c, k = i // chunk, i % chunk
+            span = slice(k * tokens, (k + 1) * tokens)
             _, l, o = merged(
-                mlbuf[d, 0, 0:1, span], mlbuf[d, 0, 1:2, span],
-                obuf[d, 0, :, span].astype(f32), *own_parts[i],
+                mlbuf[d, 0, c, 0:1, span], mlbuf[d, 0, c, 1:2, span],
+                obuf[d, 0, c, :, span].astype(f32), *own_parts[i],
             )
             h = d * half_heads + i
             att[:, h * HEAD_SIZE : (h + 1) * HEAD_SIZE] = (o / l).T.astype(bf16)
@@ -545,10 +558,10 @@
             for c in range(2):
                 h_copy(d, s, c).wait_send()
                 r_copy(d, s + 1, c).wait_send()
+                for copy in o_copies(d, s + 1, c):
+                    copy.wait_send()
             q_copy(d, s).wait_send()
             kv_copy(d, s).wait_send()
-            for c in o_copies(d, s + 1):
-                c.wait_send()
         return carry
 
     lax.fori_loop(0, n - 1, sent, 0)
@@ -563,7 +576,7 @@
     heads_here = QUERY_HEADS // n
     tokens, width = hidden.shape[1:]
     kv_cols = key_value_weight.shape[2]
-    if heads_here % 2 or kv_cols % (2 * HEAD_SIZE) or KEY_VALUE_HEADS % (n // 2) or n % 2 or tokens % 32 or width % 256:
+    if heads_here % 4 or kv_cols % (2 * HEAD_SIZE) or KEY_VALUE_HEADS % (n // 2) or n % 2 or tokens % 32 or width % 256:
         return on_device_plain(
             hidden, norm_gain, w_query, key_value_weight, w_out, cache_pages, prefix_len,
             page_owner,
@@ -609,8 +622,8 @@
             pltpu.VMEM((tokens, q_cols + kv_cols), f32),
             pltpu.VMEM((tokens, 1), f32),
             pltpu.VMEM((2, n, rows, HEAD_SIZE), bf16),
-            pltpu.VMEM((2, n, HEAD_SIZE, rows), bf16),
-            pltpu.VMEM((2, n, 2, rows), f32),
+            pltpu.VMEM((2, n, 2, HEAD_SIZE, rows // 2), bf16),
+            pltpu.VMEM((2, n, 2, 2, rows // 2), f32),
             pltpu.VMEM((2, HEAD_SIZE, rows), f32),
             pltpu.VMEM((2, 8, rows), f32),
             pltpu.VMEM((2, n, tokens, kv_cols // 2), bf16),
@@ -620,8 +633,8 @@
             pltpu.VMEM((2, tokens, half), bf16),
             dma((4,)),
         ]
-        + [dma((2, n))] * 8
-        + [dma((2, n, 2))] * 4
+        + [dma((2, n))] * 4
+        + [dma((2, n, 2))] * 8
         + [dma((2,))] * 2,
         compiler_params=pltpu.CompilerParams(
             collective_id=0, has_side_effects=True, vmem_limit_bytes=VMEM_BYTES

time: 126 us -> 126 us (level)
  no operation moved by 1% of the time
where the time goes in v3:
time: 126 us
  Pallas kernels  118 us (94%)
  local copies, waits for them, and re-layouts  4.68 us (4%)
  between operations  1.32 us (1%)
  other arithmetic  1.28 us (1%)
    pallas_call x1, Pallas kernels, on_device(): pl.pallas_call(functools.partial(layer_kernel, n, sections, heads_here),...  118 us

profile of v3, /device:TPU:1, one launch (start us, length us, event | category | flops | bytes accessed | tf_op | source)
XLA Modules:
  0.0 125.9 jit_solution(3630589782884270776)
XLA Ops:
  1.3 0.3 fusion
  1.6 0.8 pad_maximum_fusion
  2.4 1.0 broadcast_in_dim.14.bias_ref
  3.4 0.0 copy-start
  3.4 118.4 %shard_map.95 = (bf16[128,1024]{1,0:T(8,128)(2,1)}, bf16[128,2048]{1,0:T(8,128)(2,1)}) custom-call(bf16[128,1024]{1,0:T(8,128)(2,1)} %bitcast.23, f32[1,8192]{1,0:T(1,128)} %gain_ref.1, f32[128,128]{1,0:T(8,128)} %get-tuple-element.9.cos_ref, f32[128,128]{1,0:T(8,128)} %get-tuple-element.10.sin_ref, f32[1024,128]{1,0:T(8,128)} %broadcast_in_dim.14.bias_ref, ...), custom_call_target="tpu_custom_call" | custom-call | tf_op jit(solution)/shard_map/pallas_call | solution.py:607
  121.8 1.3 %reshape.29 = bf16[16,16384]{1,0:T(8,128)(2,1)S(1)} reshape(bf16[128,2048]{1,0:T(8,128)(2,1)} %get-tuple-element.5) | data formatting | bytes 1048576 | tf_op jit(solution)/shard_map/reshape | solution.py:71
  123.1 0.0 copy-done
  123.1 0.2 convert_reduce_fusion
  123.3 0.2 convolution_convert_fusion
  123.5 0.7 copy.12
  124.2 1.7 %copy.15 = bf16[1,128,1024]{2,1,0:T(8,128)(2,1)} copy(bf16[1,128,1024]{2,1,0:T(8,128)(2,1)} %bitcast.24) | data formatting | bytes 524288
  (4 shorter events, 0.0 us)
Async XLA Ops:
  3.4 119.7 %copy-start = (s32[1,16]{1,0:T(1,128)S(1)}, s32[1,16]{1,0:T(1,128)}, u32[]{:S(2)}) copy-start(s32[1,16]{1,0:T(1,128)} %param.15) | copy-start | bytes 196

commit v4 on v2

--- a/solution.py
+++ b/solution.py
@@ -196,6 +196,7 @@
     kv_half = kv_cols // 2
     key_cols = KEY_VALUE_HEADS * HEAD_SIZE
     rows = half_heads * tokens
+    wide = bias_ref.shape[1]
     group = QUERY_HEADS // KEY_VALUE_HEADS
 
     me = lax.axis_index("tp")
@@ -414,8 +415,8 @@
             values_t = vt[pl.ds(first, HEAD_SIZE), :]
             bias = bias_ref[...]
             parts = [
-                partial(keys, values_t, qbuf[d, s, r : r + tokens, :], bias)
-                for r in range(0, rows, tokens)
+                partial(keys, values_t, qbuf[d, s, r : r + wide, :], bias)
+                for r in range(0, rows, wide)
             ]
 
             @pl.when(s > 1)
@@ -424,7 +425,7 @@
                     c.wait_recv()
 
             for i, (m, l, o) in enumerate(parts):
-                span = slice(i * tokens, (i + 1) * tokens)
+                span = slice(i * wide, (i + 1) * wide)
 
                 @pl.when(s == 0)
                 def _():
@@ -563,7 +564,7 @@
     heads_here = QUERY_HEADS // n
     tokens, width = hidden.shape[1:]
     kv_cols = key_value_weight.shape[2]
-    if heads_here % 2 or kv_cols % (2 * HEAD_SIZE) or KEY_VALUE_HEADS % (n // 2) or n % 2 or tokens % 32 or width % 256:
+    if heads_here % 4 or kv_cols % (2 * HEAD_SIZE) or KEY_VALUE_HEADS % (n // 2) or n % 2 or tokens % 32 or width % 256:
         return on_device_plain(
             hidden, norm_gain, w_query, key_value_weight, w_out, cache_pages, prefix_len,
             page_owner,
@@ -584,7 +585,7 @@
     slot_at = me * slots + jnp.arange(slots, dtype=jnp.int32)
     bias = jnp.broadcast_to(
         jnp.where(slot_at < cached_len, 0.0, NEG_FILL).astype(jnp.float32)[:, None],
-        (slots, tokens),
+        (slots, 2 * tokens),
     )
     bf16, f32 = jnp.bfloat16, jnp.float32
     q_cols = heads_here * HEAD_SIZE

time: 126 us -> 126 us (level)
  no operation moved by 1% of the time
where the time goes in v4:
time: 126 us
  Pallas kernels  118 us (94%)
  local copies, waits for them, and re-layouts  4.87 us (4%)
  between operations  1.32 us (1%)
  other arithmetic  1.28 us (1%)
    pallas_call x1, Pallas kernels, on_device(): pl.pallas_call(functools.partial(layer_kernel, n, sections, heads_here),...  118 us

profile of v4, /device:TPU:1, one launch (start us, length us, event | category | flops | bytes accessed | tf_op | source)
XLA Modules:
  0.0 126.0 jit_solution(16475416197942221777)
XLA Ops:
  1.3 0.3 fusion
  1.6 0.8 pad_maximum_fusion
  2.4 1.2 broadcast_in_dim.14.bias_ref
  3.6 0.0 copy-start
  3.6 118.3 %shard_map.95 = (bf16[128,1024]{1,0:T(8,128)(2,1)}, bf16[128,2048]{1,0:T(8,128)(2,1)}) custom-call(bf16[128,1024]{1,0:T(8,128)(2,1)} %bitcast.23, f32[1,8192]{1,0:T(1,128)} %gain_ref.1, f32[128,128]{1,0:T(8,128)} %get-tuple-element.9.cos_ref, f32[128,128]{1,0:T(8,128)} %get-tuple-element.10.sin_ref, f32[1024,256]{1,0:T(8,128)} %broadcast_in_dim.14.bias_ref, ...), custom_call_target="tpu_custom_call" | custom-call | tf_op jit(solution)/shard_map/pallas_call | solution.py:595
  121.9 1.3 %reshape.29 = bf16[16,16384]{1,0:T(8,128)(2,1)S(1)} reshape(bf16[128,2048]{1,0:T(8,128)(2,1)} %get-tuple-element.5) | data formatting | bytes 1048576 | tf_op jit(solution)/shard_map/reshape | solution.py:71
  123.2 0.0 copy-done
  123.2 0.2 convert_reduce_fusion
  123.4 0.2 convolution_convert_fusion
  123.6 0.7 copy.12
  124.4 1.7 %copy.15 = bf16[1,128,1024]{2,1,0:T(8,128)(2,1)} copy(bf16[1,128,1024]{2,1,0:T(8,128)(2,1)} %bitcast.24) | data formatting | bytes 524288
  (4 shorter events, 0.0 us)
Async XLA Ops:
  3.6 119.6 %copy-start = (s32[1,16]{1,0:T(1,128)S(1)}, s32[1,16]{1,0:T(1,128)}, u32[]{:S(2)}) copy-start(s32[1,16]{1,0:T(1,128)} %param.15) | copy-start | bytes 196

commit v5 on v2

--- a/solution.py
+++ b/solution.py
@@ -184,7 +184,7 @@
     handed_ref, fresh_ref,
     wq, wkv, wo, cache, vt, hbuf, acc, sumsq, qbuf, obuf, mlbuf, own_o, own_ml, kvbuf, att,
     rbuf, upd, landed,
-    w_sem, q_send, q_recv, kv_send, kv_recv, o_send, o_recv, ml_send, ml_recv,
+    w_sem, wq_sem, wkv_sem, q_send, q_recv, kv_send, kv_recv, o_send, o_recv, ml_send, ml_recv,
     h_send, h_recv, r_send, r_recv, x_send, x_recv,
 ):
     f32, bf16 = jnp.float32, jnp.bfloat16
@@ -221,11 +221,24 @@
     loads = [
         pltpu.make_async_copy(src, dst, w_sem.at[i])
         for i, (src, dst) in enumerate(
-            ((wq_hbm, wq), (wkv_hbm, wkv), (cache_hbm, cache), (wo_hbm, wo))
+            ((cache_hbm, cache), (wo_hbm, wo))
         )
     ]
-    loads[0].start()
-    loads[1].start()
+
+    def weight_loads(d, s):
+        span = pl.ds(pl.multiple_of(owner_at(d, s) * width + d * half, 128), half)
+        return (
+            pltpu.make_async_copy(wq_hbm.at[span], wq.at[span], wq_sem.at[d, s]),
+            pltpu.make_async_copy(wkv_hbm.at[span], wkv.at[span], wkv_sem.at[d, s]),
+        )
+
+    def load_weights(s, carry):
+        for d in range(2):
+            for copy in weight_loads(d, s):
+                copy.start()
+        return carry
+
+    lax.fori_loop(0, n, load_weights, 0)
 
     sec = lax.axis_index("section")
     sec_next = lax.rem(sec + 1, sections)
@@ -277,7 +290,7 @@
 
         @pl.when(s == n - turns)
         def _():
-            loads[2].wait()
+            loads[0].wait()
 
         @pl.when(s >= n - turns)
         def _():
@@ -289,12 +302,12 @@
 
         @pl.when(s == 0)
         def _():
-            loads[0].wait()
-            loads[1].wait()
-            loads[2].start()
-            loads[3].start()
+            loads[0].start()
+            loads[1].start()
 
         for d in range(2):
+            for copy in weight_loads(d, s):
+                copy.wait()
             first = pl.multiple_of(owner_at(d, s) * width + d * half, 128)
             part = hbuf[d, s].astype(f32)
             sumsq[...] += jnp.sum(part * part, axis=1, keepdims=True)
@@ -485,7 +498,7 @@
             h = d * half_heads + i
             att[:, h * HEAD_SIZE : (h + 1) * HEAD_SIZE] = (o / l).T.astype(bf16)
 
-    loads[3].wait()
+    loads[1].wait()
 
     def r_between(d, s, t, c):
         span = pl.ds(c * piece, piece)
@@ -618,9 +631,9 @@
             pltpu.VMEM((2, n, tokens, half), bf16),
             pltpu.VMEM((2, tokens, half), bf16),
             pltpu.VMEM((2, tokens, half), bf16),
-            dma((4,)),
+            dma((2,)),
         ]
-        + [dma((2, n))] * 8
+        + [dma((2, n))] * 10
         + [dma((2, n, 2))] * 4
         + [dma((2,))] * 2,
         compiler_params=pltpu.CompilerParams(

time: 126 us -> 123 us (0.976)
  Pallas kernels: 118 us -> 116 us
    pallas_call x1, Pallas kernels: 118 us -> 116 us  [on_device(): pl.pallas_call(functools.partial(layer_kernel, n, sections, heads_here),...]
where the time goes in v5:
time: 123 us
  Pallas kernels  116 us (94%)
  local copies, waits for them, and re-layouts  4.68 us (4%)
  between operations  1.32 us (1%)
  other arithmetic  1.28 us (1%)
    pallas_call x1, Pallas kernels, on_device(): pl.pallas_call(functools.partial(layer_kernel, n, sections, heads_here),...  116 us

profile of v5, /device:TPU:1, one launch (start us, length us, event | category | flops | bytes accessed | tf_op | source)
XLA Modules:
  0.0 123.1 jit_solution(1805864114880104757)
XLA Ops:
  1.3 0.3 fusion
  1.6 0.8 pad_maximum_fusion
  2.4 1.0 broadcast_in_dim.14.bias_ref
  3.4 0.0 copy-start
  3.4 115.6 %shard_map.95 = (bf16[128,1024]{1,0:T(8,128)(2,1)}, bf16[128,2048]{1,0:T(8,128)(2,1)}) custom-call(bf16[128,1024]{1,0:T(8,128)(2,1)} %bitcast.23, f32[1,8192]{1,0:T(1,128)} %gain_ref.1, f32[128,128]{1,0:T(8,128)} %get-tuple-element.9.cos_ref, f32[128,128]{1,0:T(8,128)} %get-tuple-element.10.sin_ref, f32[1024,128]{1,0:T(8,128)} %broadcast_in_dim.14.bias_ref, ...), custom_call_target="tpu_custom_call" | custom-call | tf_op jit(solution)/shard_map/pallas_call | solution.py:607
  119.0 1.3 %reshape.29 = bf16[16,16384]{1,0:T(8,128)(2,1)S(1)} reshape(bf16[128,2048]{1,0:T(8,128)(2,1)} %get-tuple-element.5) | data formatting | bytes 1048576 | tf_op jit(solution)/shard_map/reshape | solution.py:71
  120.2 0.0 copy-done
  120.3 0.2 convert_reduce_fusion
  120.4 0.2 convolution_convert_fusion
  120.7 0.7 copy.12
  121.4 1.7 %copy.15 = bf16[1,128,1024]{2,1,0:T(8,128)(2,1)} copy(bf16[1,128,1024]{2,1,0:T(8,128)(2,1)} %bitcast.24) | data formatting | bytes 524288
  (4 shorter events, 0.0 us)
Async XLA Ops:
  3.4 116.9 %copy-start = (s32[1,16]{1,0:T(1,128)S(1)}, s32[1,16]{1,0:T(1,128)}, u32[]{:S(2)}) copy-start(s32[1,16]{1,0:T(1,128)} %param.15) | copy-start | bytes 196
